TPU v7x, 256 devices: a whole 4x4x8 slice. The times are simulated.
256 devices in a mesh: gx: 4 (over z_hi), gy: 4 (over x), gz: 16 (over z_lo, y, core).
Axes of the slice: x: 4, y: 4, z: 8 (z_hi: 4, z_lo: 2; z = z_hi * 2 + z_lo), core: 2. Of those that a mesh axis runs over, the one named last changes fastest.
Arguments:
- vectors: bfloat16 [16, 64, 2048, 128], P('gx', 'gy', 'gz'), may hold values from -0.5 to 0.5
- diag_shift: float32 [2, 16, 64, 2048], P(None, 'gx', 'gy', 'gz'), may hold values from 0.5 to 2
- coupling: float32 [16, 64, 2048], P('gx', 'gy', 'gz'), may hold values from -0.4 to 0.4
- counts: int32 [256], P(('gx', 'gy', 'gz')), may hold values from 16 to 48, as said below
Outputs:
- coarse_rows: float32 [16384, 448], P(('gx', 'gy'))
- panel: float32 [16384, 512], P(('gx', 'gy', 'gz'))
Inputs may be any that keep to these rules, and one draw needn't show every extreme that they name: `counts`: some subdomain uses 3 * 16 vectors and some uses 64 // 4.
All inputs are finite; a program needn't handle non-finite values.
Results may differ from a plain program's by a relative error of at most 0.0003.
Values may be sent and summed in bfloat16 or wider, within the bound.
A program may use at most 64 MiB of HBM per device.

v0:
```python
import jax
import jax.numpy as jnp
from jax import lax
from jax.experimental import pallas as pl
from jax.experimental.pallas import tpu as pltpu
from jax.sharding import PartitionSpec as P

F = jnp.float32
BF = jnp.bfloat16
CX, CY, CZ = 4, 16, 128
KS = 64
KL = 48
PSUB = 8
NGX, NGY, NGZ = 4, 4, 16
GROUP = 16
MESH = pl.DeviceIdType.MESH


def remote(src, dst, send, recv, device):
    return pltpu.make_async_remote_copy(
        src_ref=src, dst_ref=dst, send_sem=send, recv_sem=recv, device_id=device, device_id_type=MESH
    )


def lanes_of(x, c):
    return jnp.broadcast_to(x[:, c : c + 1], (8, 128))


def rows_of(x, r):
    return jnp.broadcast_to(x[r : r + 1, :], (8, 128))


def eliminate(A):
    rows = lax.broadcasted_iota(jnp.int32, (8, 128), 0)
    n = KL // 8
    for first in range(0, KL, GROUP):
        copies = [[None] * n for _ in range(GROUP)]
        for c in range(GROUP):
            for i in range(first // 8, n):
                copies[c][i] = lanes_of(A[i][0], first + c)
        p = rows_of(copies[0][first // 8], 0)
        for c in range(GROUP):
            J, s = (first + c) // 8, c % 8
            if c + 1 < GROUP:
                ahead = rows_of(copies[c + 1][(first + c + 1) // 8], (c + 1) % 8)
            r = lax.rsqrt(p)
            row = [rows_of(a, s) * r for a in A[J]]
            beside = [rows_of(copies[k][J], s) * r for k in range(c + 1, GROUP)]
            if c + 1 < GROUP:
                p = ahead - beside[0] * beside[0]
            for i in range(J, n):
                f = copies[c][i] * r
                if i == J:
                    f = jnp.where(rows > s, f, 0.0)
                for q in range(len(row)):
                    A[i][q] = A[i][q] - f * row[q]
                for k in range(c + 1, GROUP):
                    copies[k][i] = copies[k][i] - f * beside[k - c - 1]
            for q in range(len(row)):
                A[J][q] = jnp.where(rows == s, row[q], A[J][q])
    return A


def split3(x):
    h = x.astype(BF)
    x = x - h.astype(F)
    m = x.astype(BF)
    x = x - m.astype(F)
    return h, m, x.astype(BF)


TN = (((0,), (0,)), ((), ()))


def outer_gram(M):
    h, m, low = split3(M)
    left1 = jnp.concatenate([h[:, :KS], h[:, :KS], m[:, :KS]], 0)
    right1 = jnp.concatenate([h, m, h], 0)
    left2 = jnp.concatenate([m[:, :KS], h[:, :KS], low[:, :KS]], 0)
    right2 = jnp.concatenate([m, low, h], 0)
    return lax.dot_general(left1, right1, TN, preferred_element_type=F) + lax.dot_general(
        left2, right2, TN, preferred_element_type=F
    )


def kernel(
    cnt_ref, m_hbm, s_hbm, c_hbm, out, panel_ref,
    m, tt, sh, cp, xr, yr, zs, zr, part, partr, lead, rhs, xs, sub, gath,
    load, xsend, xrecv, ysend, yrecv, zsend, zrecv, psend, precv, lsend, lrecv, esend, erecv, rsend, rrecv,
):
    gx, gy, gz = lax.axis_index("gx"), lax.axis_index("gy"), lax.axis_index("gz")
    has = {
        "xm": gx > 0, "xp": gx < NGX - 1,
        "ym": gy > 0, "yp": gy < NGY - 1,
        "zm": gz > 0, "zp": gz < NGZ - 1,
    }
    beside = {
        "xm": {"gx": gx - 1}, "xp": {"gx": gx + 1},
        "ym": {"gy": gy - 1}, "yp": {"gy": gy + 1},
        "zm": {"gz": gz - 1}, "zp": {"gz": gz + 1},
    }
    half = CY // 2
    fetch = {}
    for k, (x, h) in enumerate([(3, 0), (0, 1), (3, 1), (0, 0), (2, None), (1, None)]):
        part_of = (x,) if h is None else (x, pl.ds(half * h, half))
        fetch[x, h] = pltpu.make_async_copy(m_hbm.at[part_of], m.at[part_of], load.at[k])
        fetch[x, h].start()
    fetch_s = pltpu.make_async_copy(s_hbm, sh, load.at[6])
    fetch_c = pltpu.make_async_copy(c_hbm, cp, load.at[7])
    fetch_s.start()
    fetch_c.start()

    barrier = pltpu.get_barrier_semaphore()
    core = lax.rem(gz, 2)
    partner = lax.rem(gz + 8, NGZ)
    sibling = gz + 1 - 2 * core
    plane = 8 * (gz // 8)
    ring = lambda k: plane + lax.rem(gz - plane + 2 * k, 8)
    up, opposite, down = ring(1), ring(2), ring(3)
    line0 = (gx == 0) & (gy == 0)
    line_y = (gx == 0) & (gy == 1)
    line_x = (gx == 1) & (gy == 0)
    leader = line0 & (gz < PSUB)
    chained = (line0 & (gz <= PSUB)) | ((line_y | line_x) & (gz < PSUB))

    also = lambda c: lax.rem(c + 8, NGZ)
    around = (up, down, opposite)
    for t in (partner, sibling) + around + tuple(also(t) for t in around):
        pl.semaphore_signal(barrier, inc=1, device_id={"gz": t}, device_id_type=MESH)
    peers = 8
    for side in has:
        @pl.when(has[side])
        def _():
            pl.semaphore_signal(barrier, inc=1, device_id=beside[side], device_id_type=MESH)

        peers = peers + has[side].astype(jnp.int32)
    for t in range(PSUB):
        @pl.when(chained & jnp.logical_not(line0 & (gz == t)))
        def _():
            pl.semaphore_signal(barrier, inc=1, device_id={"gx": 0, "gy": 0, "gz": t}, device_id_type=MESH)
    peers = peers + jnp.where(leader, 3 * PSUB, 0)

    count = cnt_ref[0]
    r128 = lax.broadcasted_iota(jnp.int32, (128, 128), 0)
    l128 = lax.broadcasted_iota(jnp.int32, (128, 128), 1)
    live_rows = (jnp.where(r128 >= KS, r128 - KS, r128) < count).astype(F).astype(BF)
    live_lanes = (jnp.where(l128 >= KS, l128 - KS, l128) < count)[:KS]

    inner_z = jnp.where(lax.broadcasted_iota(jnp.int32, (KL, 128), 1) < CZ - 1, 1.0, 0.0)

    def transpose(x, y):
        t = jnp.swapaxes(m[x, y], 0, 1) * live_rows
        tt[x, y, 0:KL] = t[0:KL]
        tt[x, y, KL : 2 * KL] = t[KS : KS + KL]

    def image(x, y):
        wide = (KL, 128)
        a0 = jnp.broadcast_to(sh[0, x, y : y + 1, :] + 6.0, wide)
        a1 = jnp.broadcast_to(sh[1, x, y : y + 1, :] + 6.0, wide)
        c = jnp.broadcast_to(cp[x, y : y + 1, :], wide)
        u = tt[x, y, 0:KL, :].astype(F)
        v = tt[x, y, KL : 2 * KL, :].astype(F)

        def forward(w, at):
            n = pltpu.roll(w, CZ - 1, 1) * inner_z
            if y < CY - 1:
                n = n + tt[x, y + 1, at : at + KL, :].astype(F)
            if x < CX - 1:
                n = n + tt[x + 1, y, at : at + KL, :].astype(F)
            return n

        yu = a0 * u + c * v - 2.0 * forward(u, 0)
        yv = a1 * v + c * u - 2.0 * forward(v, KL)
        high = [w.astype(BF) for w in (yu, yv)]
        return jnp.concatenate(high + [(w - h.astype(F)).astype(BF) for w, h in zip((yu, yv), high)], 0)

    def stage(tx, yx, G, ys=range(0, CY, 2)):
        for y in ys:
            if tx is not None:
                transpose(tx, y)
                transpose(tx, y + 1)
            if yx is not None:
                left = jnp.concatenate([image(yx, y), image(yx, y + 1)], 1)
                right = jnp.concatenate([m[yx, y], m[yx, y + 1]], 0)
                G = G + jnp.dot(left, right, preferred_element_type=F)
        return G

    x_up = remote(tt.at[3, pl.ds(0, half)], xr.at[0], xsend.at[0], xrecv.at[0], beside["xp"])
    x_down = remote(tt.at[0, pl.ds(half, half)], xr.at[1], xsend.at[1], xrecv.at[1], beside["xm"])
    y_up = remote(tt.at[:, CY - 1], yr.at[0], ysend.at[0], yrecv.at[0], beside["yp"])
    y_down = remote(tt.at[:, 0], yr.at[1], ysend.at[1], yrecv.at[1], beside["ym"])
    z_up = remote(zs.at[1], zr.at[0], zsend.at[0], zrecv.at[0], beside["zp"])
    z_down = remote(zs.at[0], zr.at[1], zsend.at[1], zrecv.at[1], beside["zm"])
    p_up = remote(part.at[1], partr.at[0], psend.at[0], precv.at[0], beside["xp"])
    p_down = remote(part.at[0], partr.at[1], psend.at[1], precv.at[1], beside["xm"])
    ways = [
        ("xp", x_up), ("xm", x_down), ("yp", y_up), ("ym", y_down),
        ("zp", z_up), ("zm", z_down), ("xp", p_up), ("xm", p_down),
    ]

    def start(side, copy):
        @pl.when(has[side])
        def _():
            copy.start()

    def arrived(side, copy, buffer, slot):
        @pl.when(has[side])
        def _():
            copy.wait_recv()

        @pl.when(jnp.logical_not(has[side]))
        def _():
            buffer[slot] = jnp.zeros(buffer.shape[1:], buffer.dtype)

    G = jnp.zeros((4 * KL, 128), F)
    lower_y, upper_y = range(0, half, 2), range(half, CY, 2)
    fetch[3, 0].wait()
    stage(3, None, G, lower_y)
    pl.semaphore_wait(barrier, peers)
    start("xp", x_up)
    fetch[0, 1].wait()
    stage(0, None, G, upper_y)
    start("xm", x_down)
    fetch[3, 1].wait()
    stage(3, None, G, upper_y)
    fetch[0, 0].wait()
    stage(0, None, G, lower_y)
    fetch[2, None].wait()
    fetch_s.wait()
    fetch_c.wait()
    G = stage(2, 3, G)
    fetch[1, None].wait()
    for x in range(CX):
        low = m[x, :, 0:16, :].astype(F)[:, 0, :]
        high = m[x, :, CZ - 16 : CZ, :].astype(F)[:, 15, :]
        ok = live_lanes[:CY]
        zs[0, CY * x : CY * (x + 1)] = jnp.where(ok, low, 0.0).astype(BF)
        zs[1, CY * x : CY * (x + 1)] = jnp.where(ok, high, 0.0).astype(BF)
    start("zp", z_up)
    start("zm", z_down)
    G = stage(1, 2, G)
    start("yp", y_up)
    start("ym", y_down)
    G = stage(None, 1, G)
    G = stage(None, 0, G)
    G = G[: 2 * KL] + G[2 * KL :]

    def both(g):
        return jnp.where(live_lanes[:KL, :KS], g[:KL, :KS] + g[KL : 2 * KL, KS:], 0.0)

    def flip(b):
        wide = jnp.concatenate([b, jnp.zeros((KL, KS), F)], 1)
        wide = jnp.concatenate([wide, jnp.zeros((128 - KL, 128), F)], 0)
        return jnp.transpose(wide)[:KL, :KS]

    C = both(G)
    C = 0.5 * (C + flip(C))
    r48 = lax.broadcasted_iota(jnp.int32, (KL, KS), 0)
    l48 = lax.broadcasted_iota(jnp.int32, (KL, KS), 1)
    C = jnp.where((r48 == l48) & (r48 >= count), 1.0, C)

    def both_z(g):
        return -(g[:KL, :KS] + g[KS : KS + KL, KS:])

    arrived("zm", z_up, zr, 0)
    arrived("zp", z_down, zr, 1)
    zp = both_z(lax.dot_general(zs[1], zr[1], TN, preferred_element_type=F))

    mine = lead.at[jnp.minimum(gz, PSUB - 1)]
    mine_sem = lrecv.at[jnp.minimum(gz, PSUB - 1)]
    along = [
        (t, remote(mine, mine, lsend.at[t], mine_sem, {"gx": 0, "gy": 0, "gz": t})) for t in range(PSUB + 1)
    ]
    for k, (ox, oy) in enumerate([(0, 1), (1, 0)]):
        along += [
            (None, remote(mine, mine, lsend.at[(k + 1) * PSUB + 1 + t], mine_sem, {"gx": ox, "gy": oy, "gz": t}))
            for t in range(PSUB)
        ]

    @pl.when(leader)
    def _():
        lead[jnp.minimum(gz, PSUB - 1)] = jnp.concatenate([C, zp], 1)
        for t, copy in along:
            if t is None:
                copy.start()
            else:
                pl.when(gz != t)(copy.start)

    zmT = both_z(lax.dot_general(zr[0], zs[0], TN, preferred_element_type=F))
    zpT = both_z(lax.dot_general(zr[1], zs[1], TN, preferred_element_type=F))

    def face(tiles, own):
        left = jnp.concatenate(tiles, 1)
        right = jnp.concatenate(own, 0)
        return -both(jnp.dot(left, right, preferred_element_type=F))

    arrived("ym", y_up, yr, 0)
    arrived("yp", y_down, yr, 1)
    ymT = face([yr[0, x] for x in range(CX)], [m[x, 0] for x in range(CX)])
    ypT = face([yr[1, x] for x in range(CX)], [m[x, CY - 1] for x in range(CX)])

    def pack(k, a, b):
        gath[gz, k] = jnp.where(core == 1, jnp.concatenate([b, a], 1), jnp.concatenate([a, b], 1))

    zero = jnp.zeros((KL, KS), F)
    pack(0, C, ymT)
    pack(1, ypT, zpT)

    class Gather:
        def __init__(self, at, send, recv, steps):
            give = lambda c, t, k: remote(at(c), at(c), send.at[k], recv.at[c], {"gz": t})
            number = iter(range(15))
            self.steps = [(waits, [give(c, t, next(number)) for c, t in pairs]) for waits, pairs in steps]
            self.sends = [s for _, sends in self.steps for s in sends]
            self.wait = lambda c: remote(at(c), at(c), send.at[0], recv.at[c], {"gz": partner}).wait_recv()

        def step(self, k):
            waits, sends = self.steps[k]
            if len(waits) == len(sends):
                for c, s in zip(waits, sends):
                    self.wait(c)
                    s.start()
                return
            for c in waits:
                self.wait(c)
            for s in sends:
                s.start()

    mine_all = (gz, partner) + around + tuple(also(t) for t in around)
    of_sibling = [t + 1 - 2 * core for t in mine_all]
    far = [also(t) for t in around]
    early = Gather(
        lambda c: gath.at[c, pl.ds(0, 2)], esend, erecv,
        [
            ([], [(gz, t) for t in (partner,) + around + (sibling,)]),
            ([partner], [(partner, t) for t in around + (sibling,)]),
            (list(around), [(t, sibling) for t in around]),
            (far, [(t, sibling) for t in far]),
            (of_sibling, []),
        ],
    )
    late = Gather(
        lambda c: gath.at[c, 2], rsend, rrecv,
        [
            ([], [(gz, t) for t in (partner,) + around + tuple(far) + (sibling,)]),
            ([partner] + list(around) + far, [(t, sibling) for t in [partner] + list(around) + far]),
            (of_sibling, []),
        ],
    )
    early.step(0)

    eye = jnp.where(r48 == l48, 1.0, 0.0)
    for i in range(PSUB):
        b = jnp.where(line0 & (gz == i), C, zero)
        b = jnp.where(line0 & (gz == i - 1), zpT, b)
        b = jnp.where(line0 & (gz == i + 1), zmT, b)
        b = jnp.where((line_y | line_x) & (gz == i), eye, b)
        rhs[i] = b
        xs[i] = zero
    sub[...] = jnp.zeros((KL, 128), F)

    r16 = lax.broadcasted_iota(jnp.int32, (KS - KL, NGZ * KS), 0) + KL
    l16 = lax.rem(lax.broadcasted_iota(jnp.int32, (KS - KL, NGZ * KS), 1), KS)
    out[KL:KS, :] = jnp.where(r16 == l16, 1.0, 0.0)
    for b in range(1, 7):
        out[KS * b + KL : KS * (b + 1), :] = jnp.zeros((KS - KL, NGZ * KS), F)

    def step(i, _):
        @pl.when(jnp.logical_not(line0 & (gz == i)))
        def _():
            remote(lead.at[i], lead.at[i], lsend.at[0], lrecv.at[i], {"gz": partner}).wait_recv()

        g = sub[...]
        a1 = lead[i] - jnp.concatenate([g[:, :KS], zero], 1)
        a2 = jnp.concatenate([rhs[i] - g[:, KS:], zero], 1)
        A = eliminate([[a1[8 * k : 8 * k + 8], a2[8 * k : 8 * k + 8]] for k in range(KL // 8)])
        a1 = jnp.concatenate([a[0] for a in A], 0)
        a2 = jnp.concatenate([a[1] for a in A], 0)
        xs[i] = a2[:, :KS]
        sub[...] = outer_gram(jnp.concatenate([a1[:, KS:], a2[:, :KS]], 1))[:KL]
        return 0

    def chain(low, high):
        @pl.when(chained)
        def _():
            lax.fori_loop(low, high, step, 0)

    chain(0, 1)
    early.step(1)
    chain(1, 3)
    early.step(2)
    arrived("xm", x_up, xr, 0)
    arrived("xp", x_down, xr, 1)
    low = face([xr[0, y] for y in range(half)], [m[0, y] for y in range(half)])
    high = face([xr[1, y] for y in range(half)], [m[CX - 1, half + y] for y in range(half)])
    part[0] = jnp.concatenate([flip(low), zero], 1)
    part[1] = jnp.concatenate([flip(high), zero], 1)
    start("xp", p_up)
    start("xm", p_down)
    early.step(3)
    chain(3, 6)
    arrived("xm", p_up, partr, 0)
    arrived("xp", p_down, partr, 1)
    xmT = low + partr[0, :, :KS]
    pack(2, xmT, high + partr[1, :, :KS])
    late.step(0)
    chain(6, PSUB)

    left = lax.broadcasted_iota(jnp.int32, (KL, 128), 1) < KS

    def lay(p, k, a, b):
        first, second = gath[2 * p, k], gath[2 * p + 1, k]
        cols = slice(128 * p, 128 * (p + 1))
        out[KS * a : KS * a + KL, cols] = jnp.where(left, first, second)
        out[KS * b : KS * b + KL, cols] = pltpu.roll(jnp.where(left, second, first), KS, 1)

    early.step(4)
    for p in range(NGZ // 2):
        lay(p, 0, 0, 3)
        lay(p, 1, 4, 6)
        below = gath[2 * p - 1, 1] if p > 0 else jnp.zeros((KL, 128), F)
        both_below = jnp.where(left, below, gath[2 * p, 1])
        turned = jnp.transpose(jnp.concatenate([both_below, jnp.zeros((128 - KL, 128), F)], 0))
        out[KS * 5 : KS * 5 + KL, 128 * p : 128 * (p + 1)] = jnp.concatenate(
            [turned[:KL, :KS], turned[KS : KS + KL, :KS]], 1
        )

    r64 = lax.broadcasted_iota(jnp.int32, (KS, KS), 0)
    l64 = lax.broadcasted_iota(jnp.int32, (KS, KS), 1)
    dead = jnp.where((r64 == l64) & (r64 >= KL), 1.0, 0.0)
    panel_ref[...] = jnp.zeros((KS, PSUB * KS), F)

    @pl.when(chained)
    def _():
        own = jnp.concatenate([jnp.where(line_y, ymT, xmT), jnp.zeros((KS - KL, KS), F)], 0)
        gap = jnp.zeros((KS - KL, KS), F)
        for p in range(PSUB // 2):
            tops = jnp.concatenate([xs[2 * p], gap, xs[2 * p + 1], gap], 0)
            times = jnp.dot(tops, own, precision=lax.Precision.HIGHEST, preferred_element_type=F)
            tops = jnp.where(line0, tops, times)
            tops = jnp.concatenate([tops, jnp.zeros((128, KS), F)], 1)
            ends = jnp.concatenate(
                [jnp.where(line0 & (gz == 2 * p + k), dead, jnp.zeros((KS, KS), F)) for k in range(2)], 1
            )
            panel_ref[:, 128 * p : 128 * (p + 1)] = jnp.transpose(tops)[:KS] + ends

    late.step(1)
    late.step(2)
    for p in range(NGZ // 2):
        lay(p, 2, 1, 2)

    for s in early.sends + late.sends:
        s.wait_send()
    for side, copy in ways:
        @pl.when(has[side])
        def _():
            copy.wait_send()

    @pl.when(leader)
    def _():
        for t, copy in along:
            if t is None:
                copy.wait_send()
            else:
                pl.when(gz != t)(copy.wait_send)


def local(vectors, diag_shift, coupling, counts):
    dma = pltpu.SemaphoreType.DMA
    columns, panel = pl.pallas_call(
        kernel,
        out_shape=(
            jax.ShapeDtypeStruct((7 * KS, NGZ * KS), F),
            jax.ShapeDtypeStruct((KS, PSUB * KS), F),
        ),
        in_specs=[pl.BlockSpec(memory_space=pltpu.SMEM)] + [pl.BlockSpec(memory_space=pltpu.HBM)] * 3,
        out_specs=(pl.BlockSpec(memory_space=pltpu.VMEM), pl.BlockSpec(memory_space=pltpu.VMEM)),
        scratch_shapes=[
            pltpu.VMEM((CX, CY, CZ, 128), BF),
            pltpu.VMEM((CX, CY, 2 * KL, CZ), BF),
            pltpu.VMEM((2, CX, CY, CZ), F),
            pltpu.VMEM((CX, CY, CZ), F),
            pltpu.VMEM((2, CY // 2, 2 * KL, CZ), BF),
            pltpu.VMEM((2, CX, 2 * KL, CZ), BF),
            pltpu.VMEM((2, CX * CY, 128), BF),
            pltpu.VMEM((2, CX * CY, 128), BF),
            pltpu.VMEM((2, KL, 128), F),
            pltpu.VMEM((2, KL, 128), F),
            pltpu.VMEM((PSUB, KL, 128), F),
            pltpu.VMEM((PSUB, KL, KS), F),
            pltpu.VMEM((PSUB, KL, KS), F),
            pltpu.VMEM((KL, 128), F),
            pltpu.VMEM((NGZ, 3, KL, 128), F),
            dma((8,)),
            dma((2,)), dma((2,)), dma((2,)), dma((2,)), dma((2,)), dma((2,)), dma((2,)), dma((2,)),
            dma((3 * PSUB + 1,)), dma((PSUB,)), dma((15,)), dma((NGZ,)), dma((15,)), dma((NGZ,)),
        ],
        compiler_params=pltpu.CompilerParams(
            collective_id=0, has_side_effects=True, vmem_limit_bytes=(50 << 20) + (100 << 10)
        ),
    )(counts, vectors, diag_shift, coupling)
    return columns.T, panel


def solution(mesh):
    return jax.shard_map(
        local,
        mesh=mesh,
        in_specs=(
            P("gx", "gy", "gz", None),
            P(None, "gx", "gy", "gz"),
            P("gx", "gy", "gz"),
            P(("gx", "gy", "gz")),
        ),
        out_specs=(P(("gx", "gy"), None), P(("gx", "gy", "gz"), None)),
        check_vma=False,
    )
```

profile of v0, /device:TPU:5, one launch (start us, length us, event | category | flops | bytes accessed | tf_op | source)
XLA Modules:
  0.0 39.4 jit_solution(13039407019823276050)
XLA Ops:
  1.3 0.0 copy-start
  1.3 0.8 %copy-done = f32[2,4,16,128]{3,2,1,0:T(8,128)S(1)} copy-done((f32[2,4,16,128]{3,2,1,0:T(8,128)S(1)}, f32[2,4,16,128]{3,2,1,0:T(8,128)}, u32[]{:S(2)}) %copy-start) | copy-done | bytes 65560
  2.1 0.0 copy-start.1
  2.1 0.8 %copy-done.1 = f32[4,16,128]{2,1,0:T(8,128)S(1)} copy-done((f32[4,16,128]{2,1,0:T(8,128)S(1)}, f32[4,16,128]{2,1,0:T(8,128)}, u32[]{:S(2)}) %copy-start.1) | copy-done | bytes 32792
  2.9 34.6 %shard_map.59 = (f32[448,1024]{1,0:T(8,128)S(1)}, f32[64,512]{1,0:T(8,128)S(1)}) custom-call(s32[1]{0:T(128)S(6)} %copy.8.cnt_ref, bf16[4,16,128,128]{3,2,1,0:T(8,128)(2,1)} %m_hbm.1, f32[2,4,16,128]{3,2,1,0:T(8,128)S(1)} %copy-done, f32[4,16,128]{2,1,0:T(8,128)S(1)} %copy-done.1), custom_call_target="tpu_custom_call" | custom-call | tf_op jit(solution)/shard_map/pallas_call | solution.py:470
  37.5 1.2 %copy.9 = f32[1024,448]{0,1:T(8,128)} copy(f32[1024,448]{0,1:T(8,128)S(1)} %bitcast.1) | data formatting | bytes 3670016
  38.7 0.7 %copy.10 = f32[64,512]{1,0:T(8,128)} copy(f32[64,512]{1,0:T(8,128)S(1)} %get-tuple-element.9) | data formatting | bytes 262144
Async XLA Ops:
  1.3 0.8 %copy-start = (f32[2,4,16,128]{3,2,1,0:T(8,128)S(1)}, f32[2,4,16,128]{3,2,1,0:T(8,128)}, u32[]{:S(2)}) copy-start(f32[2,4,16,128]{3,2,1,0:T(8,128)} %s_hbm.1) | copy-start | bytes 196612
  2.1 0.8 %copy-start.1 = (f32[4,16,128]{2,1,0:T(8,128)S(1)}, f32[4,16,128]{2,1,0:T(8,128)}, u32[]{:S(2)}) copy-start(f32[4,16,128]{2,1,0:T(8,128)} %c_hbm.1) | copy-start | bytes 98308
where the time goes:
time: 39.6 us; the launch traced here: 39.4 us
  Pallas kernels  34.6 us (87%)
  local copies, waits for them, and re-layouts  3.48 us (9%)
  between operations  1.3 us (3%)
    pallas_call x1, Pallas kernels, local(): pl.pallas_call(kernel, out_shape=(jax.ShapeDtypeStruct((7 * KS, NGZ * KS)...  34.6 us
    unnamed x6, local copies, waits for them, and re-layouts  3.48 us

commit v1 on v0

--- a/solution.py
+++ b/solution.py
@@ -72,21 +72,20 @@
 TN = (((0,), (0,)), ((), ()))
 
 
-def outer_gram(M):
-    h, m, low = split3(M)
-    left1 = jnp.concatenate([h[:, :KS], h[:, :KS], m[:, :KS]], 0)
-    right1 = jnp.concatenate([h, m, h], 0)
-    left2 = jnp.concatenate([m[:, :KS], h[:, :KS], low[:, :KS]], 0)
-    right2 = jnp.concatenate([m, low, h], 0)
+def outer_gram(W, X):
+    wh, wm, wl = split3(W)
+    h, m, low = split3(X)
+    left1, right1 = jnp.concatenate([wh, wh, wm], 0), jnp.concatenate([h, m, h], 0)
+    left2, right2 = jnp.concatenate([wm, wh, wl], 0), jnp.concatenate([m, low, h], 0)
     return lax.dot_general(left1, right1, TN, preferred_element_type=F) + lax.dot_general(
         left2, right2, TN, preferred_element_type=F
     )
 
 
 def kernel(
-    cnt_ref, m_hbm, s_hbm, c_hbm, out, panel_ref,
-    m, tt, sh, cp, xr, yr, zs, zr, part, partr, lead, rhs, xs, sub, gath,
-    load, xsend, xrecv, ysend, yrecv, zsend, zrecv, psend, precv, lsend, lrecv, esend, erecv, rsend, rrecv,
+    cnt_ref, m_hbm, s_hbm, out, panel_ref,
+    m, tt, sh, xr, yr, zs, zr, part, partr, lead, rhs, xs, sub, gath, post, postr,
+    ready, load, xsend, xrecv, ysend, yrecv, zsend, zrecv, psend, precv, lsend, lrecv, osend, orecv, esend, erecv, rsend, rrecv,
 ):
     gx, gy, gz = lax.axis_index("gx"), lax.axis_index("gy"), lax.axis_index("gz")
     has = {
@@ -99,17 +98,6 @@
         "ym": {"gy": gy - 1}, "yp": {"gy": gy + 1},
         "zm": {"gz": gz - 1}, "zp": {"gz": gz + 1},
     }
-    half = CY // 2
-    fetch = {}
-    for k, (x, h) in enumerate([(3, 0), (0, 1), (3, 1), (0, 0), (2, None), (1, None)]):
-        part_of = (x,) if h is None else (x, pl.ds(half * h, half))
-        fetch[x, h] = pltpu.make_async_copy(m_hbm.at[part_of], m.at[part_of], load.at[k])
-        fetch[x, h].start()
-    fetch_s = pltpu.make_async_copy(s_hbm, sh, load.at[6])
-    fetch_c = pltpu.make_async_copy(c_hbm, cp, load.at[7])
-    fetch_s.start()
-    fetch_c.start()
-
     barrier = pltpu.get_barrier_semaphore()
     core = lax.rem(gz, 2)
     partner = lax.rem(gz + 8, NGZ)
@@ -121,24 +109,34 @@
     line_y = (gx == 0) & (gy == 1)
     line_x = (gx == 1) & (gy == 0)
     leader = line0 & (gz < PSUB)
-    chained = (line0 & (gz <= PSUB)) | ((line_y | line_x) & (gz < PSUB))
+    chained = line0 & (gz <= PSUB)
+    follower = (line_y | line_x) & (gz < PSUB)
 
     also = lambda c: lax.rem(c + 8, NGZ)
     around = (up, down, opposite)
     for t in (partner, sibling) + around + tuple(also(t) for t in around):
         pl.semaphore_signal(barrier, inc=1, device_id={"gz": t}, device_id_type=MESH)
     peers = 8
-    for side in has:
+    for side, other in (("xp", "xm"), ("ym", "ym"), ("yp", "yp"), ("zm", "zm"), ("zp", "zp")):
         @pl.when(has[side])
         def _():
             pl.semaphore_signal(barrier, inc=1, device_id=beside[side], device_id_type=MESH)
 
-        peers = peers + has[side].astype(jnp.int32)
+        peers = peers + has[other].astype(jnp.int32)
     for t in range(PSUB):
-        @pl.when(chained & jnp.logical_not(line0 & (gz == t)))
-        def _():
-            pl.semaphore_signal(barrier, inc=1, device_id={"gx": 0, "gy": 0, "gz": t}, device_id_type=MESH)
-    peers = peers + jnp.where(leader, 3 * PSUB, 0)
+        @pl.when(chained & (gz != t))
+        def _():
+            pl.semaphore_signal(barrier, inc=1, device_id={"gz": t}, device_id_type=MESH)
+    peers = peers + jnp.where(leader, PSUB, 0)
+
+    half = CY // 2
+    fetch = {}
+    for k, (x, h) in enumerate([(3, 0), (0, 1), (3, 1), (0, 0), (2, None), (1, None)]):
+        part_of = (x,) if h is None else (x, pl.ds(half * h, half))
+        fetch[x, h] = pltpu.make_async_copy(m_hbm.at[part_of], m.at[part_of], load.at[k])
+        fetch[x, h].start()
+    fetch_s = pltpu.make_async_copy(s_hbm, sh, load.at[6])
+    fetch_s.start()
 
     count = cnt_ref[0]
     r128 = lax.broadcasted_iota(jnp.int32, (128, 128), 0)
@@ -157,7 +155,7 @@
         wide = (KL, 128)
         a0 = jnp.broadcast_to(sh[0, x, y : y + 1, :] + 6.0, wide)
         a1 = jnp.broadcast_to(sh[1, x, y : y + 1, :] + 6.0, wide)
-        c = jnp.broadcast_to(cp[x, y : y + 1, :], wide)
+        c = jnp.broadcast_to(sh[2, x, y : y + 1, :], wide)
         u = tt[x, y, 0:KL, :].astype(F)
         v = tt[x, y, KL : 2 * KL, :].astype(F)
 
@@ -216,19 +214,33 @@
     lower_y, upper_y = range(0, half, 2), range(half, CY, 2)
     fetch[3, 0].wait()
     stage(3, None, G, lower_y)
-    pl.semaphore_wait(barrier, peers)
-    start("xp", x_up)
+
+    @pl.when(has["xm"])
+    def _():
+        pl.semaphore_wait(barrier, peers)
+        pl.semaphore_signal(ready, inc=1, device_id=beside["xm"], device_id_type=MESH)
+
     fetch[0, 1].wait()
     stage(0, None, G, upper_y)
     start("xm", x_down)
+
+    @pl.when(has["xm"] & has["xp"])
+    def _():
+        pl.semaphore_wait(ready, 1)
+        x_up.start()
+
     fetch[3, 1].wait()
     stage(3, None, G, upper_y)
     fetch[0, 0].wait()
     stage(0, None, G, lower_y)
     fetch[2, None].wait()
     fetch_s.wait()
-    fetch_c.wait()
     G = stage(2, 3, G)
+
+    @pl.when(jnp.logical_not(has["xm"]))
+    def _():
+        pl.semaphore_wait(barrier, peers)
+
     fetch[1, None].wait()
     for x in range(CX):
         low = m[x, :, 0:16, :].astype(F)[:, 0, :]
@@ -268,23 +280,18 @@
 
     mine = lead.at[jnp.minimum(gz, PSUB - 1)]
     mine_sem = lrecv.at[jnp.minimum(gz, PSUB - 1)]
-    along = [
-        (t, remote(mine, mine, lsend.at[t], mine_sem, {"gx": 0, "gy": 0, "gz": t})) for t in range(PSUB + 1)
-    ]
-    for k, (ox, oy) in enumerate([(0, 1), (1, 0)]):
-        along += [
-            (None, remote(mine, mine, lsend.at[(k + 1) * PSUB + 1 + t], mine_sem, {"gx": ox, "gy": oy, "gz": t}))
-            for t in range(PSUB)
-        ]
+    along = [remote(mine, mine, lsend.at[t], mine_sem, {"gz": t}) for t in range(PSUB + 1)]
 
     @pl.when(leader)
     def _():
         lead[jnp.minimum(gz, PSUB - 1)] = jnp.concatenate([C, zp], 1)
-        for t, copy in along:
-            if t is None:
-                copy.start()
-            else:
-                pl.when(gz != t)(copy.start)
+        for t in range(PSUB + 1):
+            pl.when(gz != t)(along[t].start)
+
+    @pl.when(jnp.logical_not(has["xm"]))
+    def _():
+        pl.semaphore_wait(ready, 1)
+        x_up.start()
 
     zmT = both_z(lax.dot_general(zr[0], zs[0], TN, preferred_element_type=F))
     zpT = both_z(lax.dot_general(zr[1], zs[1], TN, preferred_element_type=F))
@@ -351,13 +358,12 @@
 
     eye = jnp.where(r48 == l48, 1.0, 0.0)
     for i in range(PSUB):
-        b = jnp.where(line0 & (gz == i), C, zero)
-        b = jnp.where(line0 & (gz == i - 1), zpT, b)
-        b = jnp.where(line0 & (gz == i + 1), zmT, b)
-        b = jnp.where((line_y | line_x) & (gz == i), eye, b)
-        rhs[i] = b
-        xs[i] = zero
-    sub[...] = jnp.zeros((KL, 128), F)
+        b = jnp.where(gz == i, C, zero)
+        b = jnp.where(gz == i - 1, zpT, b)
+        b = jnp.where(gz == i + 1, zmT, b)
+        rhs[i] = jnp.concatenate([b, jnp.where(gz == i, eye, zero)], 1)
+        xs[i] = jnp.zeros((KL, 128), F)
+    sub[...] = jnp.zeros((KL, 256), F)
 
     r16 = lax.broadcasted_iota(jnp.int32, (KS - KL, NGZ * KS), 0) + KL
     l16 = lax.rem(lax.broadcasted_iota(jnp.int32, (KS - KL, NGZ * KS), 1), KS)
@@ -365,19 +371,22 @@
     for b in range(1, 7):
         out[KS * b + KL : KS * (b + 1), :] = jnp.zeros((KS - KL, NGZ * KS), F)
 
+    first_lanes = lax.broadcasted_iota(jnp.int32, (KL, 128), 1) < KS
+
     def step(i, _):
-        @pl.when(jnp.logical_not(line0 & (gz == i)))
+        @pl.when(gz != i)
         def _():
             remote(lead.at[i], lead.at[i], lsend.at[0], lrecv.at[i], {"gz": partner}).wait_recv()
 
         g = sub[...]
-        a1 = lead[i] - jnp.concatenate([g[:, :KS], zero], 1)
-        a2 = jnp.concatenate([rhs[i] - g[:, KS:], zero], 1)
+        a1 = lead[i] - jnp.where(first_lanes, g[:, :128], 0.0)
+        a2 = rhs[i] - g[:, 128:]
         A = eliminate([[a1[8 * k : 8 * k + 8], a2[8 * k : 8 * k + 8]] for k in range(KL // 8)])
         a1 = jnp.concatenate([a[0] for a in A], 0)
         a2 = jnp.concatenate([a[1] for a in A], 0)
-        xs[i] = a2[:, :KS]
-        sub[...] = outer_gram(jnp.concatenate([a1[:, KS:], a2[:, :KS]], 1))[:KL]
+        xs[i] = a2
+        turned = pltpu.roll(a1, KS, 1)
+        sub[...] = outer_gram(turned[:, :KS], jnp.concatenate([turned, a2], 1))[:KL]
         return 0
 
     def chain(low, high):
@@ -385,26 +394,43 @@
         def _():
             lax.fori_loop(low, high, step, 0)
 
-    chain(0, 1)
     early.step(1)
-    chain(1, 3)
+    chain(0, 2)
     early.step(2)
     arrived("xm", x_up, xr, 0)
+    low = face([xr[0, y] for y in range(half)], [m[0, y] for y in range(half)])
+    part[0] = jnp.concatenate([flip(low), zero], 1)
+    start("xm", p_down)
     arrived("xp", x_down, xr, 1)
-    low = face([xr[0, y] for y in range(half)], [m[0, y] for y in range(half)])
     high = face([xr[1, y] for y in range(half)], [m[CX - 1, half + y] for y in range(half)])
-    part[0] = jnp.concatenate([flip(low), zero], 1)
     part[1] = jnp.concatenate([flip(high), zero], 1)
     start("xp", p_up)
-    start("xm", p_down)
-    early.step(3)
-    chain(3, 6)
+    chain(2, 5)
     arrived("xm", p_up, partr, 0)
     arrived("xp", p_down, partr, 1)
-    xmT = low + partr[0, :, :KS]
-    pack(2, xmT, high + partr[1, :, :KS])
+    xpT = high + partr[1, :, :KS]
+    pack(2, low + partr[0, :, :KS], xpT)
     late.step(0)
-    chain(6, PSUB)
+    early.step(3)
+    chain(5, PSUB)
+
+    to_y = remote(post.at[0], postr, osend.at[0], orecv, beside["yp"])
+    to_x = remote(post.at[1], postr, osend.at[1], orecv, beside["xp"])
+
+    @pl.when(leader)
+    def _():
+        right = jnp.concatenate([flip(ypT), flip(xpT)], 1)
+        wide = [
+            jnp.dot(xs[i][:, KS : KS + KL], right, precision=lax.Precision.HIGHEST, preferred_element_type=F)
+            for i in range(PSUB)
+        ]
+        for p in range(PSUB // 2):
+            a, b = wide[2 * p], wide[2 * p + 1]
+            post[0, p] = jnp.concatenate([a[:, :KS], b[:, :KS]], 1)
+            post[1, p] = jnp.concatenate([a[:, KS:], b[:, KS:]], 1)
+        to_y.start()
+        to_x.start()
+
 
     left = lax.broadcasted_iota(jnp.int32, (KL, 128), 1) < KS
 
@@ -425,30 +451,33 @@
             [turned[:KL, :KS], turned[KS : KS + KL, :KS]], 1
         )
 
-    r64 = lax.broadcasted_iota(jnp.int32, (KS, KS), 0)
-    l64 = lax.broadcasted_iota(jnp.int32, (KS, KS), 1)
-    dead = jnp.where((r64 == l64) & (r64 >= KL), 1.0, 0.0)
+    def put_panel(p, tile, ends):
+        t = jnp.transpose(jnp.concatenate([tile, jnp.zeros((128 - KL, 128), F)], 0))
+        panel_ref[:, 128 * p : 128 * (p + 1)] = jnp.concatenate([t[:KS, :KS], t[KS:, :KS]], 1) + ends
+
     panel_ref[...] = jnp.zeros((KS, PSUB * KS), F)
 
     @pl.when(chained)
     def _():
-        own = jnp.concatenate([jnp.where(line_y, ymT, xmT), jnp.zeros((KS - KL, KS), F)], 0)
-        gap = jnp.zeros((KS - KL, KS), F)
+        r64 = lax.broadcasted_iota(jnp.int32, (KS, KS), 0)
+        l64 = lax.broadcasted_iota(jnp.int32, (KS, KS), 1)
+        dead = jnp.where((r64 == l64) & (r64 >= KL), 1.0, 0.0)
         for p in range(PSUB // 2):
-            tops = jnp.concatenate([xs[2 * p], gap, xs[2 * p + 1], gap], 0)
-            times = jnp.dot(tops, own, precision=lax.Precision.HIGHEST, preferred_element_type=F)
-            tops = jnp.where(line0, tops, times)
-            tops = jnp.concatenate([tops, jnp.zeros((128, KS), F)], 1)
-            ends = jnp.concatenate(
-                [jnp.where(line0 & (gz == 2 * p + k), dead, jnp.zeros((KS, KS), F)) for k in range(2)], 1
-            )
-            panel_ref[:, 128 * p : 128 * (p + 1)] = jnp.transpose(tops)[:KS] + ends
+            ends = [jnp.where(gz == 2 * p + k, dead, jnp.zeros((KS, KS), F)) for k in range(2)]
+            tile = jnp.concatenate([xs[2 * p][:, :KS], xs[2 * p + 1][:, :KS]], 1)
+            put_panel(p, tile, jnp.concatenate(ends, 1))
 
     late.step(1)
     late.step(2)
     for p in range(NGZ // 2):
         lay(p, 2, 1, 2)
 
+    @pl.when(follower)
+    def _():
+        to_y.wait_recv()
+        for p in range(PSUB // 2):
+            put_panel(p, postr[p], 0.0)
+
     for s in early.sends + late.sends:
         s.wait_send()
     for side, copy in ways:
@@ -458,11 +487,10 @@
 
     @pl.when(leader)
     def _():
-        for t, copy in along:
-            if t is None:
-                copy.wait_send()
-            else:
-                pl.when(gz != t)(copy.wait_send)
+        to_y.wait_send()
+        to_x.wait_send()
+        for t in range(PSUB + 1):
+            pl.when(gz != t)(along[t].wait_send)
 
 
 def local(vectors, diag_shift, coupling, counts):
@@ -473,13 +501,12 @@
             jax.ShapeDtypeStruct((7 * KS, NGZ * KS), F),
             jax.ShapeDtypeStruct((KS, PSUB * KS), F),
         ),
-        in_specs=[pl.BlockSpec(memory_space=pltpu.SMEM)] + [pl.BlockSpec(memory_space=pltpu.HBM)] * 3,
+        in_specs=[pl.BlockSpec(memory_space=pltpu.SMEM)] + [pl.BlockSpec(memory_space=pltpu.HBM)] * 2,
         out_specs=(pl.BlockSpec(memory_space=pltpu.VMEM), pl.BlockSpec(memory_space=pltpu.VMEM)),
         scratch_shapes=[
             pltpu.VMEM((CX, CY, CZ, 128), BF),
             pltpu.VMEM((CX, CY, 2 * KL, CZ), BF),
-            pltpu.VMEM((2, CX, CY, CZ), F),
-            pltpu.VMEM((CX, CY, CZ), F),
+            pltpu.VMEM((3, CX, CY, CZ), F),
             pltpu.VMEM((2, CY // 2, 2 * KL, CZ), BF),
             pltpu.VMEM((2, CX, 2 * KL, CZ), BF),
             pltpu.VMEM((2, CX * CY, 128), BF),
@@ -487,18 +514,21 @@
             pltpu.VMEM((2, KL, 128), F),
             pltpu.VMEM((2, KL, 128), F),
             pltpu.VMEM((PSUB, KL, 128), F),
-            pltpu.VMEM((PSUB, KL, KS), F),
-            pltpu.VMEM((PSUB, KL, KS), F),
-            pltpu.VMEM((KL, 128), F),
+            pltpu.VMEM((PSUB, KL, 128), F),
+            pltpu.VMEM((PSUB, KL, 128), F),
+            pltpu.VMEM((KL, 256), F),
             pltpu.VMEM((NGZ, 3, KL, 128), F),
-            dma((8,)),
+            pltpu.VMEM((2, PSUB // 2, KL, 128), F),
+            pltpu.VMEM((PSUB // 2, KL, 128), F),
+            pltpu.SemaphoreType.REGULAR,
+            dma((7,)),
             dma((2,)), dma((2,)), dma((2,)), dma((2,)), dma((2,)), dma((2,)), dma((2,)), dma((2,)),
-            dma((3 * PSUB + 1,)), dma((PSUB,)), dma((15,)), dma((NGZ,)), dma((15,)), dma((NGZ,)),
+            dma((PSUB + 1,)), dma((PSUB,)), dma((2,)), dma, dma((15,)), dma((NGZ,)), dma((15,)), dma((NGZ,)),
         ],
         compiler_params=pltpu.CompilerParams(
             collective_id=0, has_side_effects=True, vmem_limit_bytes=(50 << 20) + (100 << 10)
         ),
-    )(counts, vectors, diag_shift, coupling)
+    )(counts, vectors, jnp.concatenate([diag_shift, coupling[None]], 0))
     return columns.T, panel
 
 

time: 39.6 us -> 37 us (0.934)
  the two profiles are of different devices: /device:TPU:5 before, /device:TPU:1 now
where the time goes in v1:
time: 37 us; the launch traced here: 36.9 us
  Pallas kernels  32.8 us (89%)
  local copies, waits for them, and re-layouts  1.89 us (5%)
  between operations  1.29 us (3%)
  other arithmetic  0.87 us (2%)
    pallas_call x1, Pallas kernels, local(): pl.pallas_call(kernel, out_shape=(jax.ShapeDtypeStruct((7 * KS, NGZ * KS)...  32.8 us
    unnamed x2, local copies, waits for them, and re-layouts  1.89 us
    concatenate x1, other arithmetic, local(): jnp.concatenate([diag_shift, coupling[None]], 0)  0.87 us

profile of v1, /device:TPU:1, one launch (start us, length us, event | category | flops | bytes accessed | tf_op | source)
XLA Modules:
  0.0 36.9 jit_solution(10514056987023461735)
XLA Ops:
  1.3 0.9 %pad_maximum_fusion.s_hbm = f32[3,4,16,128]{3,2,1,0:T(8,128)S(1)} fusion(f32[1,4,16,128]{3,2,1,0:T(8,128)} %bitcast.3, f32[2,4,16,128]{3,2,1,0:T(8,128)} %param.5), kind=kLoop, calls=%fused_computation | loop fusion | flops 24576 | bytes 196608 | tf_op jit(solution)/shard_map/concatenate | solution.py:531
  2.1 32.8 %shard_map.59 = (f32[448,1024]{1,0:T(8,128)S(1)}, f32[64,512]{1,0:T(8,128)S(1)}) custom-call(s32[1]{0:T(128)S(6)} %copy.8.cnt_ref, bf16[4,16,128,128]{3,2,1,0:T(8,128)(2,1)} %m_hbm.1, f32[3,4,16,128]{3,2,1,0:T(8,128)S(1)} %pad_maximum_fusion.s_hbm), custom_call_target="tpu_custom_call" | custom-call | tf_op jit(solution)/shard_map/pallas_call | solution.py:498
  35.0 1.2 %copy.9 = f32[1024,448]{0,1:T(8,128)} copy(f32[1024,448]{0,1:T(8,128)S(1)} %bitcast.2) | data formatting | bytes 3670016
  36.2 0.7 %copy.10 = f32[64,512]{1,0:T(8,128)} copy(f32[64,512]{1,0:T(8,128)S(1)} %get-tuple-element.9) | data formatting | bytes 262144

commit v2 on v1

--- a/solution.py
+++ b/solution.py
@@ -349,7 +349,7 @@
     late = Gather(
         lambda c: gath.at[c, 2], rsend, rrecv,
         [
-            ([], [(gz, t) for t in (partner,) + around + tuple(far) + (sibling,)]),
+            ([], [(gz, t) for t in tuple(far) + around + (partner, sibling)]),
             ([partner] + list(around) + far, [(t, sibling) for t in [partner] + list(around) + far]),
             (of_sibling, []),
         ],

time: 37 us -> 36.8 us (level)
  no operation moved by 1% of the time
where the time goes in v2:
time: 36.8 us; the launch traced here: 36.6 us
  Pallas kernels  32.6 us (89%)
  local copies, waits for them, and re-layouts  1.89 us (5%)
  between operations  1.29 us (4%)
  other arithmetic  0.87 us (2%)
    pallas_call x1, Pallas kernels, local(): pl.pallas_call(kernel, out_shape=(jax.ShapeDtypeStruct((7 * KS, NGZ * KS)...  32.6 us
    unnamed x2, local copies, waits for them, and re-layouts  1.89 us
    concatenate x1, other arithmetic, local(): jnp.concatenate([diag_shift, coupling[None]], 0)  0.87 us

profile of v2, /device:TPU:1, one launch (start us, length us, event | category | flops | bytes accessed | tf_op | source)
XLA Modules:
  0.0 36.6 jit_solution(926127994639980905)
XLA Ops:
  1.3 0.9 %pad_maximum_fusion.s_hbm = f32[3,4,16,128]{3,2,1,0:T(8,128)S(1)} fusion(f32[1,4,16,128]{3,2,1,0:T(8,128)} %bitcast.3, f32[2,4,16,128]{3,2,1,0:T(8,128)} %param.5), kind=kLoop, calls=%fused_computation | loop fusion | flops 24576 | bytes 196608 | tf_op jit(solution)/shard_map/concatenate | solution.py:531
  2.1 32.6 %shard_map.59 = (f32[448,1024]{1,0:T(8,128)S(1)}, f32[64,512]{1,0:T(8,128)S(1)}) custom-call(s32[1]{0:T(128)S(6)} %copy.8.cnt_ref, bf16[4,16,128,128]{3,2,1,0:T(8,128)(2,1)} %m_hbm.1, f32[3,4,16,128]{3,2,1,0:T(8,128)S(1)} %pad_maximum_fusion.s_hbm), custom_call_target="tpu_custom_call" | custom-call | tf_op jit(solution)/shard_map/pallas_call | solution.py:498
  34.7 1.2 %copy.9 = f32[1024,448]{0,1:T(8,128)} copy(f32[1024,448]{0,1:T(8,128)S(1)} %bitcast.2) | data formatting | bytes 3670016
  36.0 0.7 %copy.10 = f32[64,512]{1,0:T(8,128)} copy(f32[64,512]{1,0:T(8,128)S(1)} %get-tuple-element.9) | data formatting | bytes 262144

commit v3 on v2

--- a/solution.py
+++ b/solution.py
@@ -432,6 +432,10 @@
         to_x.start()
 
 
+    @pl.when(chained)
+    def _():
+        late.step(1)
+
     left = lax.broadcasted_iota(jnp.int32, (KL, 128), 1) < KS
 
     def lay(p, k, a, b):
@@ -467,7 +471,10 @@
             tile = jnp.concatenate([xs[2 * p][:, :KS], xs[2 * p + 1][:, :KS]], 1)
             put_panel(p, tile, jnp.concatenate(ends, 1))
 
-    late.step(1)
+    @pl.when(jnp.logical_not(chained))
+    def _():
+        late.step(1)
+
     late.step(2)
     for p in range(NGZ // 2):
         lay(p, 2, 1, 2)

time: 36.8 us -> 36.8 us (level)
  no operation moved by 1% of the time
where the time goes in v3:
time: 36.8 us; the launch traced here: 36.6 us
  Pallas kernels  32.6 us (89%)
  local copies, waits for them, and re-layouts  1.89 us (5%)
  between operations  1.29 us (4%)
  other arithmetic  0.87 us (2%)
    pallas_call x1, Pallas kernels, local(): pl.pallas_call(kernel, out_shape=(jax.ShapeDtypeStruct((7 * KS, NGZ * KS)...  32.6 us
    unnamed x2, local copies, waits for them, and re-layouts  1.89 us
    concatenate x1, other arithmetic, local(): jnp.concatenate([diag_shift, coupling[None]], 0)  0.87 us

profile of v3, /device:TPU:1, one launch (start us, length us, event | category | flops | bytes accessed | tf_op | source)
XLA Modules:
  0.0 36.6 jit_solution(10265848487854944657)
XLA Ops:
  1.3 0.9 %pad_maximum_fusion.s_hbm = f32[3,4,16,128]{3,2,1,0:T(8,128)S(1)} fusion(f32[1,4,16,128]{3,2,1,0:T(8,128)} %bitcast.3, f32[2,4,16,128]{3,2,1,0:T(8,128)} %param.5), kind=kLoop, calls=%fused_computation | loop fusion | flops 24576 | bytes 196608 | tf_op jit(solution)/shard_map/concatenate | solution.py:538
  2.1 32.6 %shard_map.59 = (f32[448,1024]{1,0:T(8,128)S(1)}, f32[64,512]{1,0:T(8,128)S(1)}) custom-call(s32[1]{0:T(128)S(6)} %copy.8.cnt_ref, bf16[4,16,128,128]{3,2,1,0:T(8,128)(2,1)} %m_hbm.1, f32[3,4,16,128]{3,2,1,0:T(8,128)S(1)} %pad_maximum_fusion.s_hbm), custom_call_target="tpu_custom_call" | custom-call | tf_op jit(solution)/shard_map/pallas_call | solution.py:505
  34.7 1.2 %copy.9 = f32[1024,448]{0,1:T(8,128)} copy(f32[1024,448]{0,1:T(8,128)S(1)} %bitcast.2) | data formatting | bytes 3670016
  36.0 0.7 %copy.10 = f32[64,512]{1,0:T(8,128)} copy(f32[64,512]{1,0:T(8,128)S(1)} %get-tuple-element.9) | data formatting | bytes 262144
